TPU v7x, 32 devices: a whole 2x2x4 slice. The times are simulated.
32 devices in a mesh: patch: 4 (over z), tm: 2 (over y), subject: 4 (over x, core).
Axes of the slice: x: 2, y: 2, z: 4, core: 2. Of those that a mesh axis runs over, the one named last changes fastest.
Arguments:
- frames_in: bfloat16 [32, 512, 512], P(('subject', 'patch', 'tm')), parts along dimension 0, may hold values from -6 to 6
- spatial_qkv: bfloat16 [512, 1536], replicated, may hold values from -20 to 20, as said below
- spatial_out: bfloat16 [512, 512], replicated, may hold values from -0.25 to 0.25
- temporal_qkv: bfloat16 [512, 1536], replicated, may hold values from -20 to 20, as said below
- temporal_out: bfloat16 [512, 512], replicated, may hold values from -0.25 to 0.25
Outputs:
- frames_out: bfloat16 [32, 512, 512], P(('subject', 'patch', 'tm')), parts along dimension 0
There are 4 independent parts, one for each index of `subject`. A program takes and returns all parts, laid end to end along the dimension named above; an argument that names none is the same for every part. Nothing has to cross between parts.
Inputs may be any that keep to these rules, and one draw needn't show every extreme that they name: `spatial_qkv`: columns hold query, key and value projections in that order, each 8 heads of 64. `temporal_qkv`: columns hold query, key and value projections in that order, each 8 heads of 64.
All inputs are finite; a program needn't handle non-finite values.
Results may differ from a plain program's by a relative error of at most 0.015.
Values may be sent and summed in bfloat16 or wider, within the bound.
A program may use at most 64 MiB of HBM per device.

v0:
```python
import jax
import jax.numpy as jnp
from jax import lax
from jax.sharding import PartitionSpec as P

HEADS = 8


epsilon = 1e-05
floor_score = -1e30


def layer_norm(input_rows):
    as_float = input_rows.astype(jnp.float32)
    centre = jnp.mean(as_float, axis=-1, keepdims=True)
    centered = as_float - centre
    spread = jnp.mean(centered * centered, axis=-1, keepdims=True)
    return (centered * lax.rsqrt(spread + epsilon)).astype(jnp.bfloat16)


def project_heads(input_rows, qkv_weight):
    model_width = input_rows.shape[-1]
    normed = layer_norm(input_rows)
    packed = jnp.dot(
        normed.reshape(-1, model_width), qkv_weight, preferred_element_type=jnp.float32
    ).astype(jnp.bfloat16)
    shaped = packed.reshape(input_rows.shape[:-1] + (3, HEADS, model_width // HEADS))
    return (shaped[..., 0, :, :], shaped[..., 1, :, :], shaped[..., 2, :, :])


def spatial_frame(one_frame, qkv_weight, out_weight):
    queries, key_rows, value_rows = project_heads(one_frame, qkv_weight)
    factor = queries.shape[-1] ** (-0.5)
    scores = (
        jnp.einsum("qhd,khd->hqk", queries, key_rows, preferred_element_type=jnp.float32) * factor
    )
    highest = jnp.max(scores, axis=-1, keepdims=True)
    exp_terms = jnp.exp(scores - highest)
    row_total = jnp.sum(exp_terms, axis=-1)
    mixture = jnp.einsum(
        "hqk,khd->qhd",
        exp_terms.astype(jnp.bfloat16),
        value_rows,
        preferred_element_type=jnp.float32,
    )
    mixture = (mixture / jnp.transpose(row_total)[:, :, None]).astype(jnp.bfloat16)
    update = jnp.dot(
        mixture.reshape(one_frame.shape), out_weight, preferred_element_type=jnp.float32
    )
    return (one_frame.astype(jnp.float32) + update).astype(jnp.bfloat16)


def causal_columns(columns, qkv_weight, out_weight):
    queries, key_rows, value_rows = project_heads(columns, qkv_weight)
    factor = queries.shape[-1] ** (-0.5)
    scores = (
        jnp.einsum("qchd,kchd->chqk", queries, key_rows, preferred_element_type=jnp.float32)
        * factor
    )
    frame_order = jnp.arange(columns.shape[0], dtype=jnp.int32)
    allowed = frame_order[None, :] <= frame_order[:, None]
    masked = jnp.where(allowed, scores, floor_score)
    highest = jnp.max(masked, axis=-1, keepdims=True)
    exp_terms = jnp.where(allowed, jnp.exp(masked - highest), 0.0)
    row_total = jnp.sum(exp_terms, axis=-1)
    mixture = jnp.einsum(
        "chqk,kchd->qchd",
        exp_terms.astype(jnp.bfloat16),
        value_rows,
        preferred_element_type=jnp.float32,
    )
    mixture = (mixture / jnp.transpose(row_total, (2, 0, 1))[..., None]).astype(jnp.bfloat16)
    model_width = columns.shape[-1]
    update = jnp.dot(
        mixture.reshape(-1, model_width), out_weight, preferred_element_type=jnp.float32
    )
    return (columns.astype(jnp.float32) + update.reshape(columns.shape)).astype(jnp.bfloat16)


def temporal_layer(columns, qkv_weight, out_weight):
    frame_total, column_count, model_width = columns.shape
    group_size = min(8, column_count)
    grouped = columns.reshape(
        frame_total, column_count // group_size, group_size, model_width
    ).transpose(1, 0, 2, 3)

    def group_step(group_cols):
        return causal_columns(group_cols, qkv_weight, out_weight)

    result = lax.map(group_step, grouped)
    return result.transpose(1, 0, 2, 3).reshape(frame_total, column_count, model_width)


def body(frames_in, spatial_qkv, spatial_out, temporal_qkv, temporal_out):

    def frame_step(one_frame):
        return spatial_frame(one_frame, spatial_qkv, spatial_out)

    hidden = lax.map(frame_step, frames_in)
    columns = lax.all_to_all(hidden, ("patch", "tm"), split_axis=1, concat_axis=0, tiled=True)
    result = temporal_layer(columns, temporal_qkv, temporal_out)
    return lax.all_to_all(result, ("patch", "tm"), split_axis=0, concat_axis=1, tiled=True)


def solution(mesh):
    in_specs = (P(("subject", "patch", "tm"), None, None), P(), P(), P(), P())
    out_specs = P(("subject", "patch", "tm"), None, None)
    return jax.shard_map(body, mesh=mesh, in_specs=in_specs, out_specs=out_specs, check_vma=False)
```

profile of v0, /device:TPU:0, one launch (start us, length us, event | category | flops | bytes accessed | tf_op | source)
XLA Modules:
  0.0 166.2 jit_solution(2995010740043860410)
XLA Ops:
  2.7 3.2 %convolution_convert_fusion.1 = bf16[512,1536]{1,0:T(8,128)(2,1)} fusion(bf16[512,1536]{1,0:T(8,128)(2,1)S(1)} %copy-done, bf16[1,512,512]{2,1,0:T(8,128)(2,1)} %param.7, f32[512]{0:T(512)S(1)} %add_rsqrt_fusion.1, f32[512]{0:T(512)S(1)} %broadcast_multiply_fusion.1), kind=kOutput, calls=%fused_computation.43 | convolution fusion | flops 807141376 | bytes 3674112 | tf_op jit(solution)/shard_map/while/body/eval_jaxpr/dot_general | solution.py:24
  14.8 5.6 %reduce.2 = bf16[512,512]{1,0:T(8,128)(2,1)} reduce(bf16[512,1,512]{2,1,0:T(2,128)(2,1)} %bitcast.162, bf16[]{:T(256)} %broadcast.91), dimensions={1}, to_apply=%bitcast.119.reduce_sub_computation | reduce | bytes 1048578
  20.4 2.2 %reshape.81 = bf16[8,2,16384]{2,1,0:T(2,128)(2,1)} reshape(bf16[512,512]{1,0:T(8,128)(2,1)} %reduce.2) | data formatting | bytes 1048576
  22.7 7.3 %all-to-all-start = ((bf16[8,2,16384]{2,1,0:T(2,128)(2,1)}), bf16[8,2,16384]{2,1,0:T(2,128)(2,1)}, u32[]{:S(2)}, u32[]{:S(2)}) async-start(bf16[8,2,16384]{2,1,0:T(2,128)(2,1)} %reshape.81), calls=%async_computation | async-start | bytes 1048576 | tf_op jit(solution)/shard_map/all_to_all | solution.py:100
  29.9 14.6 %all-to-all-done = bf16[8,2,16384]{2,1,0:T(2,128)(2,1)} async-done(((bf16[8,2,16384]{2,1,0:T(2,128)(2,1)}), bf16[8,2,16384]{2,1,0:T(2,128)(2,1)}, u32[]{:S(2)}, u32[]{:S(2)}) %all-to-all-start) | async-done | bytes 524320 | tf_op jit(solution)/shard_map/all_to_all | solution.py:100
  44.5 3.5 %reshape.82 = bf16[512,1,512]{2,1,0:T(2,128)(2,1)} reshape(bf16[8,2,16384]{2,1,0:T(2,128)(2,1)} %all-to-all-done) | data formatting | bytes 1048576
  48.0 2.2 %copy.52 = bf16[1,512,512]{2,1,0:T(8,128)(2,1)} copy(bf16[1,512,512]{2,0,1:T(2,128)(2,1)} %bitcast.161) | data formatting | bytes 1048576
  50.2 96.9 %while.2 = (s32[]{:T(128)}, bf16[8,8,8,512]{3,2,0,1:T(8,128)(2,1)}, bf16[8,8,8,512]{3,2,0,1:T(8,128)(2,1)}, bf16[512,1536]{1,0:T(8,128)(2,1)S(1)}, bf16[512,512]{1,0:T(8,128)(2,1)}, /*index=5*/s32[]{:T(128)}) while((s32[]{:T(128)}, bf16[8,8,8,512]{3,2,0,1:T(8,128)(2,1)}, bf16[8,8,8,512]{3,2,0,1:T(8,128)(2,1)}, ...), condition=%wide.region_9.10_spmd, body=%wide.region_4.9_spmd.sunk | while | flops 136422032 | bytes 4694661 | solution.py:90
  52.3 1.9 %convolution_convert_fusion.3 = bf16[64,1536]{1,0:T(8,128)(2,1)} fusion(bf16[512,1536]{1,0:T(8,128)(2,1)S(1)} %get-tuple-element.120, f32[64]{0:T(128)S(1)} %rsqrt.26, f32[64]{0:T(128)S(1)} %div.59, bf16[8,8,8,512]{3,2,0,1:T(8,128)(2,1)} %get-tuple-element.119, s32[]{:T(128)} %get-tuple-element.111), kind=kOutput, calls=%fused_computation.1.clone.1 | convolution fusion | flops 100892672 | bytes 1836032 | tf_op jit(solution)/shard_map/while/body/eval_jaxpr/dot_general | solution.py:24
  57.1 1.9 %fusion.75 = f32[8,8,8]{2,1,0:T(8,128)} fusion(bf16[8,8,1,8,64]{4,3,2,1,0:T(8,128)(2,1)} %copy-done.3, bf16[8,8,1,8,64]{4,3,2,1,0:T(8,128)(2,1)} %copy-done.2, pred[8,8]{0,1:T(8,128)(4,1)S(1)} %iota_compare_fusion.2), kind=kOutput, calls=%fused_computation.66.clone.1 | convolution fusion | flops 544775 | bytes 133184 | tf_op jit(solution)/shard_map/while/body/eval_jaxpr/sub | solution.py:64
  64.4 1.9 %convolution_convert_fusion.3 = bf16[64,1536]{1,0:T(8,128)(2,1)} fusion(bf16[512,1536]{1,0:T(8,128)(2,1)S(1)} %get-tuple-element.120, f32[64]{0:T(128)S(1)} %rsqrt.26, f32[64]{0:T(128)S(1)} %div.59, bf16[8,8,8,512]{3,2,0,1:T(8,128)(2,1)} %get-tuple-element.119, s32[]{:T(128)} %get-tuple-element.111), kind=kOutput, calls=%fused_computation.1.clone.1 | convolution fusion | flops 100892672 | bytes 1836032 | tf_op jit(solution)/shard_map/while/body/eval_jaxpr/dot_general | solution.py:24
  69.2 1.9 %fusion.75 = f32[8,8,8]{2,1,0:T(8,128)} fusion(bf16[8,8,1,8,64]{4,3,2,1,0:T(8,128)(2,1)} %copy-done.3, bf16[8,8,1,8,64]{4,3,2,1,0:T(8,128)(2,1)} %copy-done.2, pred[8,8]{0,1:T(8,128)(4,1)S(1)} %iota_compare_fusion.2), kind=kOutput, calls=%fused_computation.66.clone.1 | convolution fusion | flops 544775 | bytes 133184 | tf_op jit(solution)/shard_map/while/body/eval_jaxpr/sub | solution.py:64
  76.5 1.9 %convolution_convert_fusion.3 = bf16[64,1536]{1,0:T(8,128)(2,1)} fusion(bf16[512,1536]{1,0:T(8,128)(2,1)S(1)} %get-tuple-element.120, f32[64]{0:T(128)S(1)} %rsqrt.26, f32[64]{0:T(128)S(1)} %div.59, bf16[8,8,8,512]{3,2,0,1:T(8,128)(2,1)} %get-tuple-element.119, s32[]{:T(128)} %get-tuple-element.111), kind=kOutput, calls=%fused_computation.1.clone.1 | convolution fusion | flops 100892672 | bytes 1836032 | tf_op jit(solution)/shard_map/while/body/eval_jaxpr/dot_general | solution.py:24
  81.3 1.9 %fusion.75 = f32[8,8,8]{2,1,0:T(8,128)} fusion(bf16[8,8,1,8,64]{4,3,2,1,0:T(8,128)(2,1)} %copy-done.3, bf16[8,8,1,8,64]{4,3,2,1,0:T(8,128)(2,1)} %copy-done.2, pred[8,8]{0,1:T(8,128)(4,1)S(1)} %iota_compare_fusion.2), kind=kOutput, calls=%fused_computation.66.clone.1 | convolution fusion | flops 544775 | bytes 133184 | tf_op jit(solution)/shard_map/while/body/eval_jaxpr/sub | solution.py:64
  88.6 1.9 %convolution_convert_fusion.3 = bf16[64,1536]{1,0:T(8,128)(2,1)} fusion(bf16[512,1536]{1,0:T(8,128)(2,1)S(1)} %get-tuple-element.120, f32[64]{0:T(128)S(1)} %rsqrt.26, f32[64]{0:T(128)S(1)} %div.59, bf16[8,8,8,512]{3,2,0,1:T(8,128)(2,1)} %get-tuple-element.119, s32[]{:T(128)} %get-tuple-element.111), kind=kOutput, calls=%fused_computation.1.clone.1 | convolution fusion | flops 100892672 | bytes 1836032 | tf_op jit(solution)/shard_map/while/body/eval_jaxpr/dot_general | solution.py:24
  93.4 1.9 %fusion.75 = f32[8,8,8]{2,1,0:T(8,128)} fusion(bf16[8,8,1,8,64]{4,3,2,1,0:T(8,128)(2,1)} %copy-done.3, bf16[8,8,1,8,64]{4,3,2,1,0:T(8,128)(2,1)} %copy-done.2, pred[8,8]{0,1:T(8,128)(4,1)S(1)} %iota_compare_fusion.2), kind=kOutput, calls=%fused_computation.66.clone.1 | convolution fusion | flops 544775 | bytes 133184 | tf_op jit(solution)/shard_map/while/body/eval_jaxpr/sub | solution.py:64
  100.7 1.9 %convolution_convert_fusion.3 = bf16[64,1536]{1,0:T(8,128)(2,1)} fusion(bf16[512,1536]{1,0:T(8,128)(2,1)S(1)} %get-tuple-element.120, f32[64]{0:T(128)S(1)} %rsqrt.26, f32[64]{0:T(128)S(1)} %div.59, bf16[8,8,8,512]{3,2,0,1:T(8,128)(2,1)} %get-tuple-element.119, s32[]{:T(128)} %get-tuple-element.111), kind=kOutput, calls=%fused_computation.1.clone.1 | convolution fusion | flops 100892672 | bytes 1836032 | tf_op jit(solution)/shard_map/while/body/eval_jaxpr/dot_general | solution.py:24
  105.6 1.9 %fusion.75 = f32[8,8,8]{2,1,0:T(8,128)} fusion(bf16[8,8,1,8,64]{4,3,2,1,0:T(8,128)(2,1)} %copy-done.3, bf16[8,8,1,8,64]{4,3,2,1,0:T(8,128)(2,1)} %copy-done.2, pred[8,8]{0,1:T(8,128)(4,1)S(1)} %iota_compare_fusion.2), kind=kOutput, calls=%fused_computation.66.clone.1 | convolution fusion | flops 544775 | bytes 133184 | tf_op jit(solution)/shard_map/while/body/eval_jaxpr/sub | solution.py:64
  112.9 1.9 %convolution_convert_fusion.3 = bf16[64,1536]{1,0:T(8,128)(2,1)} fusion(bf16[512,1536]{1,0:T(8,128)(2,1)S(1)} %get-tuple-element.120, f32[64]{0:T(128)S(1)} %rsqrt.26, f32[64]{0:T(128)S(1)} %div.59, bf16[8,8,8,512]{3,2,0,1:T(8,128)(2,1)} %get-tuple-element.119, s32[]{:T(128)} %get-tuple-element.111), kind=kOutput, calls=%fused_computation.1.clone.1 | convolution fusion | flops 100892672 | bytes 1836032 | tf_op jit(solution)/shard_map/while/body/eval_jaxpr/dot_general | solution.py:24
  117.7 1.9 %fusion.75 = f32[8,8,8]{2,1,0:T(8,128)} fusion(bf16[8,8,1,8,64]{4,3,2,1,0:T(8,128)(2,1)} %copy-done.3, bf16[8,8,1,8,64]{4,3,2,1,0:T(8,128)(2,1)} %copy-done.2, pred[8,8]{0,1:T(8,128)(4,1)S(1)} %iota_compare_fusion.2), kind=kOutput, calls=%fused_computation.66.clone.1 | convolution fusion | flops 544775 | bytes 133184 | tf_op jit(solution)/shard_map/while/body/eval_jaxpr/sub | solution.py:64
  125.0 1.9 %convolution_convert_fusion.3 = bf16[64,1536]{1,0:T(8,128)(2,1)} fusion(bf16[512,1536]{1,0:T(8,128)(2,1)S(1)} %get-tuple-element.120, f32[64]{0:T(128)S(1)} %rsqrt.26, f32[64]{0:T(128)S(1)} %div.59, bf16[8,8,8,512]{3,2,0,1:T(8,128)(2,1)} %get-tuple-element.119, s32[]{:T(128)} %get-tuple-element.111), kind=kOutput, calls=%fused_computation.1.clone.1 | convolution fusion | flops 100892672 | bytes 1836032 | tf_op jit(solution)/shard_map/while/body/eval_jaxpr/dot_general | solution.py:24
  129.8 1.9 %fusion.75 = f32[8,8,8]{2,1,0:T(8,128)} fusion(bf16[8,8,1,8,64]{4,3,2,1,0:T(8,128)(2,1)} %copy-done.3, bf16[8,8,1,8,64]{4,3,2,1,0:T(8,128)(2,1)} %copy-done.2, pred[8,8]{0,1:T(8,128)(4,1)S(1)} %iota_compare_fusion.2), kind=kOutput, calls=%fused_computation.66.clone.1 | convolution fusion | flops 544775 | bytes 133184 | tf_op jit(solution)/shard_map/while/body/eval_jaxpr/sub | solution.py:64
  137.1 1.9 %convolution_convert_fusion.3 = bf16[64,1536]{1,0:T(8,128)(2,1)} fusion(bf16[512,1536]{1,0:T(8,128)(2,1)S(1)} %get-tuple-element.120, f32[64]{0:T(128)S(1)} %rsqrt.26, f32[64]{0:T(128)S(1)} %div.59, bf16[8,8,8,512]{3,2,0,1:T(8,128)(2,1)} %get-tuple-element.119, s32[]{:T(128)} %get-tuple-element.111), kind=kOutput, calls=%fused_computation.1.clone.1 | convolution fusion | flops 100892672 | bytes 1836032 | tf_op jit(solution)/shard_map/while/body/eval_jaxpr/dot_general | solution.py:24
  147.1 18.3 %all_to_all.21 = bf16[8,64,512]{2,1,0:T(8,128)(2,1)S(1)} all-to-all(bf16[8,64,512]{2,1,0:T(8,128)(2,1)} %bitcast.164), channel_id=1, replica_groups=mesh['patch'=4,'tm'=2,'subject'=4] {'patch','tm'}, dimensions={0} | all-to-all | bytes 1048576 | tf_op jit(solution)/shard_map/all_to_all | solution.py:102
  (166 shorter events, 80.0 us)
Async XLA Ops:
  0.0 2.7 %copy-start = (bf16[512,1536]{1,0:T(8,128)(2,1)S(1)}, bf16[512,1536]{1,0:T(8,128)(2,1)}, u32[]{:S(2)}) copy-start(bf16[512,1536]{1,0:T(8,128)(2,1)} %param.8) | copy-start | bytes 4718596
  10.3 1.6 copy-start.4
  10.3 1.6 copy-start.5
  12.4 37.7 %copy-start.1 = (bf16[512,1536]{1,0:T(8,128)(2,1)S(1)}, bf16[512,1536]{1,0:T(8,128)(2,1)}, u32[]{:S(2)}) copy-start(bf16[512,1536]{1,0:T(8,128)(2,1)} %param.10) | copy-start | bytes 4718596
  22.7 21.9 %all-to-all-start = ((bf16[8,2,16384]{2,1,0:T(2,128)(2,1)}), bf16[8,2,16384]{2,1,0:T(2,128)(2,1)}, u32[]{:S(2)}, u32[]{:S(2)}) async-start(bf16[8,2,16384]{2,1,0:T(2,128)(2,1)} %reshape.81), calls=%async_computation | async-start | bytes 1048576 | tf_op jit(solution)/shard_map/all_to_all | solution.py:100
  56.1 0.7 copy-start.2
  56.1 0.7 copy-start.3
  68.2 0.7 copy-start.2
  68.2 0.7 copy-start.3
  80.4 0.7 copy-start.2
  80.4 0.7 copy-start.3
  92.5 0.7 copy-start.2
  92.5 0.7 copy-start.3
  104.6 0.7 copy-start.2
  104.6 0.7 copy-start.3
  116.7 0.7 copy-start.2
  116.7 0.7 copy-start.3
  128.8 0.7 copy-start.2
  128.8 0.7 copy-start.3
  140.9 0.7 copy-start.2
  140.9 0.7 copy-start.3
where the time goes:
time: 169 us; the launch traced here: 166 us
  matrix products  64.3 us (38%)
  local copies, waits for them, and re-layouts  36.1 us (21%)
  other arithmetic  25.2 us (15%)
  blocking collectives  18.3 us (11%)
  waiting for transfers between devices  14.6 us (9%)
  starting transfers between devices  7.28 us (4%)
    dot_general x9, matrix products, project_heads(): jnp.dot(normed.reshape(-1, model_width), qkv_weight, preferred_element_ty...  18.8 us
    all_to_all x1, blocking collectives, body(): lax.all_to_all(result, ('patch', 'tm'), split_axis=0, concat_axis=1, tile...  18.3 us
    sub x8, matrix products, causal_columns(): exp_terms = jnp.where(allowed, jnp.exp(masked - highest), 0.0)  15.3 us
    dot_general x8, matrix products, causal_columns(): jnp.dot(mixture.reshape(-1, model_width), out_weight, preferred_element_t...  15.1 us
    all_to_all x1, waiting for transfers between devices, body(): lax.all_to_all(hidden, ('patch', 'tm'), split_axis=1, concat_axis=0, tile...  14.6 us
    dot_general x8, matrix products, causal_columns(): jnp.einsum('chqk,kchd->qchd', exp_terms.astype(jnp.bfloat16), value_rows,...  9.72 us
    reshape x8, local copies, waits for them, and re-layouts, project_heads(): packed.reshape(input_rows.shape[:-1] + (3, HEADS, model_width // HEADS))  9.49 us
    reduce_sum x9, other arithmetic, layer_norm(): spread = jnp.mean(centered * centered, axis=-1, keepdims=True)  9.36 us
  transfers between devices with their start and end apart: 1, of which 1 were waited for; matrix products, arithmetic and copies ran while one was open for 0% of the time, Pallas kernels for 0%

commit v1 on v0

v1 whole, which is shorter than its diff:
```python
import functools

import jax
import jax.numpy as jnp
from jax import lax
from jax.experimental import pallas as pl
from jax.experimental.pallas import tpu as pltpu
from jax.sharding import PartitionSpec as P

HEADS = 8
PAIR = 128
CHUNKS = 2

epsilon = 1e-05
floor_score = -1e30
MESH = pl.DeviceIdType.MESH
bf16, f32 = jnp.bfloat16, jnp.float32


def layer_norm(input_rows):
    as_float = input_rows.astype(f32)
    centre = jnp.mean(as_float, axis=-1, keepdims=True)
    centered = as_float - centre
    spread = jnp.mean(centered * centered, axis=-1, keepdims=True)
    return (centered * lax.rsqrt(spread + epsilon)).astype(bf16)


def dot(a, b):
    return jnp.dot(a, b, preferred_element_type=f32)


def dot_t(a, b):
    return lax.dot_general(a, b, (((1,), (1,)), ((), ())), preferred_element_type=f32)


def stacked_heads(q_pair, low):
    zero = jnp.zeros_like(q_pair)
    return jnp.concatenate([jnp.where(low, q_pair, zero), jnp.where(low, zero, q_pair)], axis=0)


def attend(q_pair, k_pair, v_pair, allowed):
    rows, keys = q_pair.shape[0], k_pair.shape[0]
    low = lax.broadcasted_iota(jnp.int32, (rows, PAIR), 1) < PAIR // 2
    scores = dot_t(stacked_heads(q_pair, low), k_pair)
    if allowed is not None:
        scores = jnp.where(allowed, scores, floor_score)
    highest = jnp.max(scores, axis=-1, keepdims=True)
    exp_terms = jnp.exp(scores - highest)
    if allowed is not None:
        exp_terms = jnp.where(allowed, exp_terms, 0.0)
    values = jnp.concatenate([v_pair, jnp.ones((keys, PAIR), bf16)], axis=1)
    mixed = dot(exp_terms.astype(bf16), values)
    mixed = mixed[:, :PAIR] / mixed[:, PAIR:]
    return jnp.where(low, mixed[:rows], mixed[rows:]).astype(bf16)


def fused_kernel(zs, ys, x_hbm, sqkv_hbm, sout_hbm, tqkv_hbm, tout_hbm, out_ref,
                 x, sqkv, sout, tqkv, tout, packed, hid, recv, tpacked, attn, tattn, res,
                 load_sem, own_sem, fsend, frecv, bsend, brecv):
    patches, width = x.shape
    group = zs * ys
    block = patches // group
    part = block // CHUNKS
    z, y = lax.axis_index("patch"), lax.axis_index("tm")
    me = z * ys + y
    half = zs // 2
    pairs = width // PAIR
    scale = (width // HEADS) ** -0.5

    order = []
    for j in range(zs):
        base = (z // half) * half
        if j < half:
            base = half - base
        zz = base + (z % half + j % half + (1 if j >= half else 0)) % half
        for i in range(ys):
            yy = (y + i + 1) % ys
            order.append((zz, yy, zz * ys + yy))
    peers = order[:-1]

    barrier = pltpu.get_barrier_semaphore()
    for zz, yy, _ in peers:
        pl.semaphore_signal(barrier, inc=1, device_id={"patch": zz, "tm": yy}, device_id_type=MESH)
    loads = [
        pltpu.make_async_copy(src, dst, load_sem.at[i])
        for i, (src, dst) in enumerate(
            [(x_hbm, x), (sqkv_hbm, sqkv), (sout_hbm, sout), (tqkv_hbm, tqkv), (tout_hbm, tout)]
        )
    ]
    for copy in loads:
        copy.start()

    def rows_of(d, c):
        return pl.ds(pl.multiple_of(d * block + c * part, 16), part)

    def forward(zz, yy, d, c):
        return pltpu.make_async_remote_copy(
            src_ref=hid.at[rows_of(d, c)], dst_ref=recv.at[c, me],
            send_sem=fsend.at[c, d], recv_sem=frecv.at[c, me],
            device_id={"patch": zz, "tm": yy}, device_id_type=MESH)

    def forward_in(zz, yy, d, c):
        return pltpu.make_async_remote_copy(
            src_ref=hid.at[rows_of(d, c)], dst_ref=recv.at[c, d],
            send_sem=fsend.at[c, d], recv_sem=frecv.at[c, d],
            device_id={"patch": zz, "tm": yy}, device_id_type=MESH)

    def back(zz, yy, d, c):
        return pltpu.make_async_remote_copy(
            src_ref=res.at[c, d], dst_ref=out_ref.at[rows_of(me, c)],
            send_sem=bsend.at[c, d], recv_sem=brecv.at[c, me],
            device_id={"patch": zz, "tm": yy}, device_id_type=MESH)

    def back_in(zz, yy, d, c):
        return pltpu.make_async_remote_copy(
            src_ref=res.at[c, d], dst_ref=out_ref.at[rows_of(d, c)],
            send_sem=bsend.at[c, d], recv_sem=brecv.at[c, d],
            device_id={"patch": zz, "tm": yy}, device_id_type=MESH)

    loads[0].wait()
    loads[1].wait()
    normed = layer_norm(x[...])
    packed[:, :width] = (dot(normed, sqkv[:, :width]).astype(bf16) * scale).astype(bf16)
    packed[:, width:] = dot(normed, sqkv[:, width:]).astype(bf16)
    loads[2].wait()
    pl.semaphore_wait(barrier, group - 1)

    for j in range(zs):
        zz = order[j * ys][0]
        rows = pl.ds(pl.multiple_of(zz * (ys * block), ys * block), ys * block)
        for p in range(pairs):
            lanes = slice(p * PAIR, (p + 1) * PAIR)
            attn[:, lanes] = attend(
                packed[rows, p * PAIR:(p + 1) * PAIR],
                packed[:, width + p * PAIR:width + (p + 1) * PAIR],
                packed[:, 2 * width + p * PAIR:2 * width + (p + 1) * PAIR], None)
        hid[rows, :] = (x[rows, :].astype(f32) + dot(attn[...], sout[...])).astype(bf16)
        for i in range(ys):
            zz, yy, d = order[j * ys + i]
            if j * ys + i < group - 1:
                forward(zz, yy, d, 0).start()
    for zz, yy, d in peers:
        for c in range(1, CHUNKS):
            forward(zz, yy, d, c).start()
    for c in range(CHUNKS):
        recv[c, pl.ds(me, 1)] = hid[rows_of(me, c), :].reshape(1, part, width)
    loads[3].wait()
    loads[4].wait()

    sub = 16
    keys = group * sub
    at_q = lax.broadcasted_iota(jnp.int32, (2 * keys, keys), 0) % keys
    at_k = lax.broadcasted_iota(jnp.int32, (2 * keys, keys), 1)
    allowed = (at_q % sub == at_k % sub) & (at_k // sub <= at_q // sub)
    for c in range(CHUNKS):
        for zz, yy, d in peers:
            forward_in(zz, yy, d, c).wait_recv()
        got = recv[c].reshape(group * part, width)
        normed = layer_norm(got)
        tpacked[:, :, :width] = (
            (dot(normed, tqkv[:, :width]).astype(bf16) * scale).astype(bf16).reshape(group, part, width))
        tpacked[:, :, width:] = (
            dot(normed, tqkv[:, width:]).astype(bf16).reshape(group, part, 2 * width))
        for s in range(part // sub):
            at = slice(s * sub, (s + 1) * sub)
            for p in range(pairs):
                lanes = slice(p * PAIR, (p + 1) * PAIR)
                q, k, v = (
                    tpacked[:, at, w * width + p * PAIR:w * width + (p + 1) * PAIR].reshape(keys, PAIR)
                    for w in range(3)
                )
                tattn[:, at, lanes] = attend(q, k, v, allowed).reshape(group, sub, PAIR)
        update = dot(tattn[...].reshape(group * part, width), tout[...])
        res[c] = (got.astype(f32) + update).astype(bf16).reshape(group, part, width)
        for zz, yy, d in peers:
            back(zz, yy, d, c).start()
        pltpu.make_async_copy(res.at[c, me], out_ref.at[rows_of(me, c)], own_sem.at[c]).start()

    for c in range(CHUNKS):
        for zz, yy, d in peers:
            forward(zz, yy, d, c).wait_send()
            back(zz, yy, d, c).wait_send()
            back_in(zz, yy, d, c).wait_recv()
        pltpu.make_async_copy(res.at[c, me], out_ref.at[rows_of(me, c)], own_sem.at[c]).wait()


def fused(zs, ys, frame, sqkv, sout, tqkv, tout):
    patches, width = frame.shape
    group = zs * ys
    block = patches // group
    part = block // CHUNKS
    anywhere = pl.BlockSpec(memory_space=pl.ANY)
    dma = pltpu.SemaphoreType.DMA
    return pl.pallas_call(
        functools.partial(fused_kernel, zs, ys),
        out_shape=jax.ShapeDtypeStruct((patches, width), bf16),
        in_specs=[anywhere] * 5,
        out_specs=anywhere,
        scratch_shapes=[
            pltpu.VMEM((patches, width), bf16),
            pltpu.VMEM(sqkv.shape, bf16),
            pltpu.VMEM(sout.shape, bf16),
            pltpu.VMEM(tqkv.shape, bf16),
            pltpu.VMEM(tout.shape, bf16),
            pltpu.VMEM((patches, 3 * width), bf16),
            pltpu.VMEM((patches, width), bf16),
            pltpu.VMEM((CHUNKS, group, part, width), bf16),
            pltpu.VMEM((group, part, 3 * width), bf16),
            pltpu.VMEM((ys * block, width), bf16),
            pltpu.VMEM((group, part, width), bf16),
            pltpu.VMEM((CHUNKS, group, part, width), bf16),
            dma((5,)),
            dma((CHUNKS,)),
            dma((CHUNKS, group)),
            dma((CHUNKS, group)),
            dma((CHUNKS, group)),
            dma((CHUNKS, group)),
        ],
        compiler_params=pltpu.CompilerParams(
            collective_id=0, has_side_effects=True, vmem_limit_bytes=48 * 2**20),
    )(frame, sqkv, sout, tqkv, tout)


def spatial_frame(one_frame, qkv_weight, out_weight):
    width = one_frame.shape[-1]
    scale = (width // HEADS) ** -0.5
    packed = dot(layer_norm(one_frame), qkv_weight).astype(bf16)
    queries, keys, values = jnp.split(packed, 3, axis=-1)
    queries = (queries * scale).astype(bf16)
    mixture = jnp.concatenate(
        [attend(queries[:, a:a + PAIR], keys[:, a:a + PAIR], values[:, a:a + PAIR], None)
         for a in range(0, width, PAIR)], axis=-1)
    return (one_frame.astype(f32) + dot(mixture, out_weight)).astype(bf16)


def temporal_columns(columns, qkv_weight, out_weight):
    frames, count, width = columns.shape
    scale = (width // HEADS) ** -0.5
    rows = columns.reshape(frames * count, width)
    packed = dot(layer_norm(rows), qkv_weight).astype(bf16)
    queries, keys, values = jnp.split(packed, 3, axis=-1)
    queries = (queries * scale).astype(bf16)
    place = jnp.arange(frames * count, dtype=jnp.int32)
    allowed = (place[:, None] % count == place[None, :] % count) & (
        place[None, :] // count <= place[:, None] // count)
    allowed = jnp.concatenate([allowed, allowed], axis=0)
    mixture = jnp.concatenate(
        [attend(queries[:, a:a + PAIR], keys[:, a:a + PAIR], values[:, a:a + PAIR], allowed)
         for a in range(0, width, PAIR)], axis=-1)
    return (rows.astype(f32) + dot(mixture, out_weight)).astype(bf16).reshape(columns.shape)


def solution(mesh):
    zs, ys = mesh.shape["patch"], mesh.shape["tm"]
    group = zs * ys

    def body(frames_in, spatial_qkv, spatial_out, temporal_qkv, temporal_out):
        frames, patches, width = frames_in.shape
        if frames == 1 and zs % 2 == 0 and patches % (16 * CHUNKS * group) == 0:
            return fused(zs, ys, frames_in[0], spatial_qkv, spatial_out, temporal_qkv, temporal_out)[None]
        hidden = lax.map(lambda frame: spatial_frame(frame, spatial_qkv, spatial_out), frames_in)
        columns = lax.all_to_all(hidden, ("patch", "tm"), split_axis=1, concat_axis=0, tiled=True)
        result = temporal_columns(columns, temporal_qkv, temporal_out)
        return lax.all_to_all(result, ("patch", "tm"), split_axis=0, concat_axis=1, tiled=True)

    in_specs = (P(("subject", "patch", "tm"), None, None), P(), P(), P(), P())
    out_specs = P(("subject", "patch", "tm"), None, None)
    return jax.shard_map(body, mesh=mesh, in_specs=in_specs, out_specs=out_specs, check_vma=False)
```

time: 169 us -> 37.7 us (0.22); the launches traced: 166 us -> 37.4 us
  matrix products: 64.3 us -> 0 us
  Pallas kernels: 0 us -> 30.7 us
  local copies, waits for them, and re-layouts: 36.1 us -> 6.73 us
  other arithmetic: 25.2 us -> 0 us
  blocking collectives: 18.3 us -> 0 us
  waiting for transfers between devices: 14.6 us -> 0 us
  starting transfers between devices: 7.28 us -> 0 us
    dot_general x36 -> x0, matrix products: 49.1 us -> none  [the longest x9 18.8 us: project_heads(): jnp.dot(normed.reshape(-1, model_width), qkv_weight, preferred_element_ty...]
    pallas_call x0 -> x1, Pallas kernels: none -> 30.7 us  [fused(): pl.pallas_call(functools.partial(fused_kernel, zs, ys), out_shape=jax.Sha...]
    reduce_sum x19 -> x0, other arithmetic: 19.5 us -> none  [the longest x9 9.36 us: layer_norm(): spread = jnp.mean(centered * centered, axis=-1, keepdims=True)]
    all_to_all x1 -> x0, blocking collectives: 18.3 us -> none  [body(): lax.all_to_all(result, ('patch', 'tm'), split_axis=0, concat_axis=1, tile...]
    sub x8 -> x0, matrix products: 15.3 us -> none  [causal_columns(): exp_terms = jnp.where(allowed, jnp.exp(masked - highest), 0.0)]
    all_to_all x1 -> x0, waiting for transfers between devices: 14.6 us -> none  [body(): lax.all_to_all(hidden, ('patch', 'tm'), split_axis=1, concat_axis=0, tile...]
    reshape x8 -> x0, local copies, waits for them, and re-layouts: 9.49 us -> none  [project_heads(): packed.reshape(input_rows.shape[:-1] + (3, HEADS, model_width // HEADS))]
    all_to_all x1 -> x0, starting transfers between devices: 7.28 us -> none  [body(): lax.all_to_all(hidden, ('patch', 'tm'), split_axis=1, concat_axis=0, tile...]
  transfers between devices with their start and end apart: 1 -> 0, of which waited for: 1 -> 0; matrix products, arithmetic and copies ran while one was open for 0% -> 0% of each run, Pallas kernels for 0% -> 0%
where the time goes in v1:
time: 37.7 us; the launch traced here: 37.4 us
  Pallas kernels  30.7 us (81%)
  local copies, waits for them, and re-layouts  6.73 us (18%)
    pallas_call x1, Pallas kernels, fused(): pl.pallas_call(functools.partial(fused_kernel, zs, ys), out_shape=jax.Sha...  30.7 us
    unnamed x11, local copies, waits for them, and re-layouts  6.73 us

profile of v1, /device:TPU:0, one launch (start us, length us, event | category | flops | bytes accessed | tf_op | source)
XLA Modules:
  0.0 37.4 jit_solution(4007931361009894175)
XLA Ops:
  0.0 0.0 copy-start
  0.0 1.4 %copy-done = bf16[512,1536]{1,0:T(8,128)(2,1)S(1)} copy-done((bf16[512,1536]{1,0:T(8,128)(2,1)S(1)}, bf16[512,1536]{1,0:T(8,128)(2,1)}, u32[]{:S(2)}) %copy-start) | copy-done | bytes 1572888
  1.4 0.0 copy-start.1
  1.4 1.4 %copy-done.1 = bf16[512,1536]{1,0:T(8,128)(2,1)S(1)} copy-done((bf16[512,1536]{1,0:T(8,128)(2,1)S(1)}, bf16[512,1536]{1,0:T(8,128)(2,1)}, u32[]{:S(2)}) %copy-start.1) | copy-done | bytes 1572888
  2.8 0.0 copy-start.2
  2.8 1.0 %copy-done.2 = bf16[1,512,512]{2,1,0:T(8,128)(2,1)S(1)} copy-done((bf16[1,512,512]{2,1,0:T(8,128)(2,1)S(1)}, bf16[1,512,512]{2,1,0:T(8,128)(2,1)}, u32[]{:S(2)}) %copy-start.2) | copy-done | bytes 524312
  3.9 0.0 copy-start.3
  3.9 1.0 %copy-done.3 = bf16[512,512]{1,0:T(8,128)(2,1)S(1)} copy-done((bf16[512,512]{1,0:T(8,128)(2,1)S(1)}, bf16[512,512]{1,0:T(8,128)(2,1)}, u32[]{:S(2)}) %copy-start.3) | copy-done | bytes 524312
  4.9 0.0 copy-start.4
  4.9 1.0 %copy-done.4 = bf16[512,512]{1,0:T(8,128)(2,1)S(1)} copy-done((bf16[512,512]{1,0:T(8,128)(2,1)S(1)}, bf16[512,512]{1,0:T(8,128)(2,1)}, u32[]{:S(2)}) %copy-start.4) | copy-done | bytes 524312
  5.9 30.7 %shard_map.55 = bf16[512,512]{1,0:T(8,128)(2,1)S(1)} custom-call(bf16[512,512]{1,0:T(8,128)(2,1)S(1)} %bitcast.3, bf16[512,1536]{1,0:T(8,128)(2,1)S(1)} %copy-done, bf16[512,512]{1,0:T(8,128)(2,1)S(1)} %copy-done.3, bf16[512,1536]{1,0:T(8,128)(2,1)S(1)} %copy-done.1, bf16[512,512]{1,0:T(8,128)(2,1)S(1)} %copy-done.4), custom_call_target="tpu_custom_call" | custom-call | tf_op jit(solution)/shard_map/pallas_call | solution.py:194
  36.6 0.8 %copy.7 = bf16[1,512,512]{2,1,0:T(8,128)(2,1)} copy(bf16[1,512,512]{2,1,0:T(8,128)(2,1)S(1)} %bitcast.2) | data formatting | bytes 1048576
Async XLA Ops:
  0.0 1.4 %copy-start = (bf16[512,1536]{1,0:T(8,128)(2,1)S(1)}, bf16[512,1536]{1,0:T(8,128)(2,1)}, u32[]{:S(2)}) copy-start(bf16[512,1536]{1,0:T(8,128)(2,1)} %sqkv_hbm.1) | copy-start | bytes 4718596
  1.4 1.4 %copy-start.1 = (bf16[512,1536]{1,0:T(8,128)(2,1)S(1)}, bf16[512,1536]{1,0:T(8,128)(2,1)}, u32[]{:S(2)}) copy-start(bf16[512,1536]{1,0:T(8,128)(2,1)} %tqkv_hbm.1) | copy-start | bytes 4718596
  2.8 1.0 %copy-start.2 = (bf16[1,512,512]{2,1,0:T(8,128)(2,1)S(1)}, bf16[1,512,512]{2,1,0:T(8,128)(2,1)}, u32[]{:S(2)}) copy-start(bf16[1,512,512]{2,1,0:T(8,128)(2,1)} %param.5) | copy-start | bytes 1572868
  3.9 1.0 %copy-start.3 = (bf16[512,512]{1,0:T(8,128)(2,1)S(1)}, bf16[512,512]{1,0:T(8,128)(2,1)}, u32[]{:S(2)}) copy-start(bf16[512,512]{1,0:T(8,128)(2,1)} %sout_hbm.1) | copy-start | bytes 1572868
  4.9 1.0 %copy-start.4 = (bf16[512,512]{1,0:T(8,128)(2,1)S(1)}, bf16[512,512]{1,0:T(8,128)(2,1)}, u32[]{:S(2)}) copy-start(bf16[512,512]{1,0:T(8,128)(2,1)} %tout_hbm.1) | copy-start | bytes 1572868

commit v2 on v1

--- a/solution.py
+++ b/solution.py
@@ -189,7 +189,7 @@
     group = zs * ys
     block = patches // group
     part = block // CHUNKS
-    anywhere = pl.BlockSpec(memory_space=pl.ANY)
+    anywhere = pl.BlockSpec(memory_space=pltpu.HBM)
     dma = pltpu.SemaphoreType.DMA
     return pl.pallas_call(
         functools.partial(fused_kernel, zs, ys),
@@ -217,7 +217,7 @@
             dma((CHUNKS, group)),
         ],
         compiler_params=pltpu.CompilerParams(
-            collective_id=0, has_side_effects=True, vmem_limit_bytes=48 * 2**20),
+            collective_id=0, has_side_effects=True, vmem_limit_bytes=62 * 2**20),
     )(frame, sqkv, sout, tqkv, tout)
 
 

time: 37.7 us -> 33.4 us (0.89)
  local copies, waits for them, and re-layouts: 6.73 us -> 1.87 us
  Pallas kernels: 30.7 us -> 31.4 us
    unnamed x11 -> x1, local copies, waits for them, and re-layouts: 6.73 us -> 1.87 us
    pallas_call x1, Pallas kernels: 30.7 us -> 31.4 us  [fused(): pl.pallas_call(functools.partial(fused_kernel, zs, ys), out_shape=jax.Sha...]
where the time goes in v2:
time: 33.4 us; the launch traced here: 33.3 us
  Pallas kernels  31.4 us (94%)
  local copies, waits for them, and re-layouts  1.87 us (6%)
    pallas_call x1, Pallas kernels, fused(): pl.pallas_call(functools.partial(fused_kernel, zs, ys), out_shape=jax.Sha...  31.4 us
    unnamed x1, local copies, waits for them, and re-layouts  1.87 us

profile of v2, /device:TPU:0, one launch (start us, length us, event | category | flops | bytes accessed | tf_op | source)
XLA Modules:
  0.0 33.3 jit_solution(4764820303787871569)
XLA Ops:
  0.0 31.4 %shard_map.55 = bf16[512,512]{1,0:T(8,128)(2,1)} custom-call(bf16[512,512]{1,0:T(8,128)(2,1)} %bitcast.3, bf16[512,1536]{1,0:T(8,128)(2,1)} %sqkv_hbm.1, bf16[512,512]{1,0:T(8,128)(2,1)} %sout_hbm.1, bf16[512,1536]{1,0:T(8,128)(2,1)} %tqkv_hbm.1, bf16[512,512]{1,0:T(8,128)(2,1)} %tout_hbm.1), custom_call_target="tpu_custom_call" | custom-call | tf_op jit(solution)/shard_map/pallas_call | solution.py:194
  31.4 1.9 %copy.7 = bf16[1,512,512]{2,1,0:T(8,128)(2,1)} copy(bf16[1,512,512]{2,1,0:T(8,128)(2,1)} %bitcast.2) | data formatting | bytes 1048576
